TPU v7x, 32 devices: a whole 2x2x4 slice. The times are simulated.
32 devices in a mesh: gx: 8 (over z, x), gy: 4 (over y, core).
Axes of the slice: x: 2, y: 2, z: 4, core: 2. Of those that a mesh axis runs over, the one named last changes fastest.
Arguments:
- self_block: bfloat16 [16, 4, 2, 128, 128], P('gx', 'gy'), may hold values from -6 to 6
- coupling: bfloat16 [16, 4, 4, 2, 128, 128], P('gx', 'gy'), may hold values from -6 to 6
- skeleton: int32 [16, 4, 64], P('gx', 'gy'), may hold values from 0 to 127, as said below
- redundant: int32 [16, 4, 64], P('gx', 'gy'), may hold values from 0 to 127
- interp: bfloat16 [16, 4, 2, 64, 64], P('gx', 'gy'), may hold values from -0.5 to 0.5
- pivot: int32 [16, 4, 64], P('gx', 'gy'), may hold values from 0 to 63, each once within a row
- pivot_inverse: bfloat16 [16, 4, 2, 64, 64], P('gx', 'gy'), may hold values from -0.046875 to 0.046875
Outputs:
- factor: bfloat16 [16, 4, 5, 2, 64, 128], P('gx', 'gy')
- updated_self: bfloat16 [16, 4, 2, 128, 128], P('gx', 'gy')
- coarse: bfloat16 [8, 4, 2, 128, 128], P('gx', 'gy')
Inputs may be any that keep to these rules, and one draw needn't show every extreme that they name: For each box, skeleton and redundant together list every point 0 to 127 exactly once.
All inputs are finite; a program needn't handle non-finite values.
Results may differ from a plain program's by a relative error of at most 0.0075.
Values may be sent and summed in bfloat16 or wider, within the bound.
A program may use at most 64 MiB of HBM per device.

v0:
```python
import jax
import jax.numpy as jnp
from jax import lax
from jax.sharding import PartitionSpec as P


def from_behind(value, axis, steps):
    count = lax.axis_size(axis)
    pairs = [(source, (source + steps) % count) for source in range(count)]
    return lax.ppermute(value, axis, pairs)


def padded(cells, sides, width):
    for axis, dim in sides:
        count = lax.axis_size(axis)
        head = lax.slice_in_dim(cells, 0, width, axis=dim)
        tail = lax.slice_in_dim(cells, cells.shape[dim] - width, cells.shape[dim], axis=dim)
        cells = jnp.concatenate(
            [
                lax.ppermute(tail, axis, [(i, (i + 1) % count) for i in range(count)]),
                cells,
                lax.ppermute(head, axis, [((i + 1) % count, i) for i in range(count)]),
            ],
            axis=dim,
        )
    return cells


def swapped(value, axis, distance):
    mask = 2**distance
    pairs = [(source, source ^ mask) for source in range(lax.axis_size(axis))]
    return lax.ppermute(value, axis, pairs)


def complex_product(first, second, output, left_op, right_op):
    mixed = jnp.stack(
        [
            jnp.stack([right_op[:, 0], right_op[:, 1]], 1),
            jnp.stack([-right_op[:, 1], right_op[:, 0]], 1),
        ],
        1,
    )
    form = (
        first[0]
        + "c"
        + first[1:]
        + ","
        + second[0]
        + "ce"
        + second[1:]
        + "->"
        + output[0]
        + "e"
        + output[1:]
    )
    return jnp.einsum(form, left_op, mixed, preferred_element_type=jnp.float32)


def select_rows(selector, block_in):
    return jnp.einsum(
        "bsp,bcpn->bcsn", selector, block_in, preferred_element_type=jnp.float32
    ).astype(jnp.bfloat16)


def outgoing_factor(qt_mat, pivot_inv, block_in):
    reduced = complex_product("brp", "bpn", "brn", qt_mat, block_in).astype(jnp.bfloat16)
    return complex_product("bij", "bjn", "bin", pivot_inv, reduced).astype(jnp.bfloat16)


def incoming_factor(qt_mat, block_in):
    return complex_product("brp", "bmp", "brm", qt_mat, block_in).astype(jnp.bfloat16)


def rank_update(left_t, right_op):
    return complex_product("brm", "brn", "bmn", left_t, right_op)


def prepare(skel_index, red_index, interp_blk, pivot_order, inverse, points):
    point_ids = lax.iota(jnp.int32, points)
    pick_skel = (skel_index[:, :, None] == point_ids).astype(jnp.bfloat16)
    pick_red = (red_index[:, :, None] == point_ids).astype(jnp.bfloat16)
    spread = jnp.einsum("bcsr,bsp->bcrp", interp_blk, pick_skel, preferred_element_type=jnp.float32)
    qt_mat = jnp.stack([pick_red.astype(jnp.float32) - spread[:, 0], -spread[:, 1]], 1).astype(
        jnp.bfloat16
    )
    pivot_pick = (pivot_order[:, :, None] == lax.iota(jnp.int32, pivot_order.shape[-1])).astype(
        jnp.bfloat16
    )
    pivot_inv = jnp.einsum(
        "bcai,bij->bcaj", inverse, pivot_pick, preferred_element_type=jnp.float32
    ).astype(jnp.bfloat16)
    return (pick_skel, qt_mat, pivot_inv)


def local(self_block, coupling, skeleton, redundant, interp, pivot, pivot_inverse):
    own_block = self_block[:, 0]
    couple_pairs = coupling[:, 0]
    skel_index = skeleton[:, 0]
    red_index = redundant[:, 0]
    interp_blk = interp[:, 0]
    pivot_order = pivot[:, 0]
    inverse = pivot_inverse[:, 0]
    box_count = own_block.shape[0]
    half_count = box_count // 2
    points = own_block.shape[-1]
    skel_size = skel_index.shape[-1]
    pick_skel, qt_mat, pivot_inv = prepare(
        skel_index, red_index, interp_blk, pivot_order, inverse, points
    )
    edge_pairs = from_behind(couple_pairs[box_count - 1 :, 0:2], "gx", 1)
    left_pairs = jnp.concatenate([edge_pairs, couple_pairs[:-1, 0:2]], 0)
    own_factor = outgoing_factor(qt_mat, pivot_inv, own_block)
    left_factor = outgoing_factor(qt_mat, pivot_inv, left_pairs[:, 1])
    right_factor = outgoing_factor(qt_mat, pivot_inv, couple_pairs[:, 0])
    up_factor = outgoing_factor(qt_mat, pivot_inv, couple_pairs[:, 2])
    left_term = incoming_factor(qt_mat, left_pairs[:, 0])
    right_term = incoming_factor(qt_mat, couple_pairs[:, 1])
    up_term = incoming_factor(qt_mat, couple_pairs[:, 3])
    left_update = rank_update(left_term, left_factor)
    right_update = rank_update(right_term, right_factor)
    edge_send = jnp.stack([left_update[0], right_update[box_count - 1]], 0)
    edge_recv = padded(edge_send.astype(jnp.bfloat16), (("gx", 0),), 1).astype(edge_send.dtype)
    from_left = jnp.concatenate([edge_recv[0:1], right_update[:-1]], 0)
    from_right = jnp.concatenate([left_update[1:], edge_recv[3:4]], 0)
    lower_pairs = from_behind(couple_pairs[:, 2:4], "gy", 1)
    down_factor = outgoing_factor(qt_mat, pivot_inv, lower_pairs[:, 1])
    down_term = incoming_factor(qt_mat, lower_pairs[:, 0])
    down_rows = select_rows(pick_skel, lower_pairs[:, 1])
    row_send = jnp.stack([rank_update(down_term, down_factor), rank_update(up_term, up_factor)], 1)
    row_recv = padded(row_send.astype(jnp.bfloat16), (("gy", 1),), 1).astype(row_send.dtype)
    from_below = row_recv[:, 0]
    from_above = row_recv[:, 3]
    total_blk = own_block.astype(jnp.float32) - (from_left + from_right + from_below + from_above)
    updated = total_blk.astype(jnp.bfloat16)
    row_shape = (box_count, 2, skel_size, points)
    total_rows = jnp.take_along_axis(
        total_blk, jnp.broadcast_to(skel_index[:, None, :, None], row_shape), axis=2
    )
    skel_self = select_rows(pick_skel, own_block)
    edge_zero = complex_product("bsp", "brp", "bsr", skel_self, qt_mat).astype(jnp.bfloat16)
    skel_rows = (total_rows - complex_product("bsr", "brn", "bsn", edge_zero, own_factor)).astype(
        jnp.bfloat16
    )
    lower_side = lax.axis_index("gy") % 2 == 0
    up_rows = select_rows(pick_skel, couple_pairs[:, 2])
    toward_rows = jnp.where(lower_side, up_rows, down_rows)
    toward_factor = jnp.where(lower_side, up_factor, down_factor)
    cross_rows = (
        toward_rows.astype(jnp.float32)
        - complex_product("bsr", "brn", "bsn", edge_zero, toward_factor)
    ).astype(jnp.bfloat16)
    block_shape = (box_count, 2, skel_size, skel_size)
    skel_block = jnp.take_along_axis(
        skel_rows, jnp.broadcast_to(skel_index[:, None, None, :], block_shape), axis=3
    )
    skel_packed = jnp.concatenate([skel_block[:, 0], skel_block[:, 1]], -1)
    send_pack = jnp.stack([cross_rows[:, 0], cross_rows[:, 1], skel_packed, pick_skel], 1)
    send_half = jnp.where(lower_side, send_pack[half_count:], send_pack[:half_count])
    partner_pack = swapped(send_half, "gy", 0)
    kept_cross = jnp.where(lower_side, cross_rows[:half_count], cross_rows[half_count:])
    kept_skel = jnp.where(lower_side, skel_block[:half_count], skel_block[half_count:])
    kept_pick = jnp.where(lower_side, pick_skel[:half_count], pick_skel[half_count:])
    partner_skel = jnp.stack(
        [partner_pack[:, 2, :, :skel_size], partner_pack[:, 2, :, skel_size:]], 1
    )
    own_coupling = jnp.einsum(
        "bcsp,btp->bcst", kept_cross, partner_pack[:, 3], preferred_element_type=jnp.float32
    ).astype(jnp.bfloat16)
    partner_coupling = jnp.einsum(
        "bcsp,btp->bcst", partner_pack[:, 0:2], kept_pick, preferred_element_type=jnp.float32
    ).astype(jnp.bfloat16)
    lower_skel = jnp.where(lower_side, kept_skel, partner_skel)
    upper_skel = jnp.where(lower_side, partner_skel, kept_skel)
    upper_right = jnp.where(lower_side, own_coupling, partner_coupling)
    lower_left = jnp.where(lower_side, partner_coupling, own_coupling)
    top_rows = jnp.concatenate([lower_skel, upper_right], -1)
    bottom_rows = jnp.concatenate([lower_left, upper_skel], -1)
    coarse = jnp.concatenate([top_rows, bottom_rows], -2)[:, None]
    factor = jnp.stack([own_factor, left_factor, right_factor, down_factor, up_factor], 1)[:, None]
    return (factor, updated[:, None], coarse)


def solution(mesh):
    placed = (
        P("gx", "gy", None, None, None),
        P("gx", "gy", None, None, None, None),
        P("gx", "gy", None),
        P("gx", "gy", None),
        P("gx", "gy", None, None, None),
        P("gx", "gy", None),
        P("gx", "gy", None, None, None),
    )
    return jax.shard_map(
        local,
        mesh=mesh,
        in_specs=placed,
        out_specs=(
            P("gx", "gy", None, None, None, None),
            P("gx", "gy", None, None, None),
            P("gx", "gy", None, None, None),
        ),
        check_vma=False,
    )
```

profile of v0, /device:TPU:0, one launch (start us, length us, event | category | flops | bytes accessed | tf_op | source)
XLA Modules:
  0.0 519.3 jit_solution(12180160182748748595)
XLA Ops:
  0.6 1.1 copy.358
  1.8 0.5 collective-permute-start.1
  2.3 2.6 collective-permute-start
  4.9 0.3 fusion.153
  5.3 0.2 fusion.87
  5.9 0.2 convolution_convert_fusion.2
  6.1 0.2 fusion.2
  6.6 0.4 copy-done.5
  7.2 0.2 fusion.57
  8.7 0.2 fusion.53
  9.1 0.2 fusion.49
  10.0 1.4 collective-permute-done
  11.7 0.2 fusion.55
  12.0 0.2 fusion.31
  12.2 0.2 convolution_bitcast_fusion.2
  12.5 2.4 collective-permute-start.3
  14.9 0.2 convolution_bitcast_fusion.3
  15.3 2.0 collective-permute-done.3
  17.3 5.4 %collective-permute-done.2 = bf16[1,2,128,128]{3,2,1,0:T(8,128)(2,1)S(1)} collective-permute-done((bf16[1,2,128,128]{3,2,1,0:T(8,128)(2,1)S(1)}, bf16[1,2,128,128]{3,2,1,0:T(8,128)(2,1)S(1)}, u32[]{:S(2)}, u32[]{:S(2)}) %collective-permute-start.2) | collective-permute-done | bytes 65568 | tf_op jit(solution)/shard_map/ppermute | solution.py:20
  23.3 0.2 fusion.51
  23.6 0.2 convolution_bitcast_fusion.1
  24.3 0.2 convolution_bitcast_fusion
  24.5 1.7 collective-permute-start.5
  26.2 0.8 copy.96
  27.2 0.2 fusion.7
  27.4 0.9 collective-permute-done.4
  28.3 0.4 collective-permute-done.5
  28.8 313.0 %gather_fusion = f32[32768]{0:T(1024)S(1)} fusion(f32[2,2,128,128]{3,2,1,0:T(8,128)S(1)} %get-tuple-element.12, s32[32768]{0:T(1024)S(1)} %bitcast.464), kind=kCustom, calls=%fused_computation | custom fusion | bytes 786432 | tf_op jit(solution)/shard_map/jit(take_along_axis)/gather | solution.py:136
  341.9 173.5 %gather_fusion.1 = bf16[16384]{0:T(1024)(128)(2,1)S(1)} fusion(bf16[2,2,64,128]{3,2,1,0:T(8,128)(2,1)S(1)} %fusion.38, s32[16384]{0:T(1024)S(1)} %reshape.165), kind=kCustom, calls=%fused_computation.1 | custom fusion | bytes 327680 | tf_op jit(solution)/shard_map/jit(take_along_axis)/gather | solution.py:153
  515.8 1.5 collective-permute-start.6
  517.3 0.7 fusion.59
  518.5 0.7 maximum_bitcast_fusion.21
  (121 shorter events, 5.4 us)
Async XLA Ops:
  0.6 5.9 %copy-start = (bf16[2,1,2,64,64]{4,3,2,1,0:T(8,128)(2,1)S(1)}, bf16[2,1,2,64,64]{4,3,2,1,0:T(8,128)(2,1)}, u32[]{:S(2)}) copy-start(bf16[2,1,2,64,64]{4,3,2,1,0:T(8,128)(2,1)} %param.13) | copy-start | bytes 98308
  1.8 21.0 %collective-permute-start.1 = (bf16[2,2,2,128,128]{4,3,2,0,1:T(8,128)(2,1)S(1)}, bf16[2,2,2,128,128]{4,3,2,0,1:T(8,128)(2,1)S(1)}, u32[]{:S(2)}, u32[]{:S(2)}) collective-permute-start(bf16[2,2,2,128,128]{4,3,2,0,1:T(8,128)(2,1)S(1)} %slice.409), channel_id=1, source_target_pairs={{0,1},{1,2},{2,3},{3,0},{4,5},{5,6},{6,7},{7,4},{8,9},{9,10},{10,1... | collective-permute-start | bytes 786440 | tf_op jit(solution)/shard_map/ppermute | solution.py:10
  2.3 2.9 copy-start.3
  2.3 3.0 copy-start.2
  2.3 3.2 copy-start.4
  2.3 9.0 %collective-permute-start = (bf16[1,2,2,128,128]{4,3,2,0,1:T(8,128)(2,1)S(1)}, bf16[1,2,2,128,128]{4,3,2,0,1:T(8,128)(2,1)S(1)}, u32[]{:S(2)}, u32[]{:S(2)}) collective-permute-start(bf16[1,2,2,128,128]{4,3,2,0,1:T(8,128)(2,1)S(1)} %get-tuple-element.33), channel_id=1, source_target_pairs={{0,4},{4,8},{8,12},{12,16},{16,20},{20,24},{24,28},{28,0},{1,5},{5... | collective-permute-start | bytes 393224 | tf_op jit(solution)/shard_map/ppermute | solution.py:10
  5.2 0.9 copy-start.1
  6.3 0.7 copy-start.5
  12.5 4.8 collective-permute-start.3
  15.2 7.6 %collective-permute-start.2 = (bf16[1,2,128,128]{3,2,1,0:T(8,128)(2,1)S(1)}, bf16[1,2,128,128]{3,2,1,0:T(8,128)(2,1)S(1)}, u32[]{:S(2)}, u32[]{:S(2)}) collective-permute-start(bf16[1,2,128,128]{3,2,1,0:T(8,128)(2,1)S(1)} %slice.570), channel_id=1, source_target_pairs={{0,4},{4,8},{8,12},{12,16},{16,20},{20,24},{24,28},{28,0},{1,5},{5... | collective-permute-start | bytes 196616 | tf_op jit(solution)/shard_map/ppermute | solution.py:20
  23.9 4.4 collective-permute-start.4
  24.5 4.2 collective-permute-start.5
  515.8 2.4 collective-permute-start.6
where the time goes:
time: 519 us
  local copies, waits for them, and re-layouts  490 us (94%)
  waiting for transfers between devices  10.4 us (2%)
  starting transfers between devices  8.86 us (2%)
  matrix products  5.56 us (1%)
    gather x1, local copies, waits for them, and re-layouts, local(): jnp.take_along_axis(total_blk, jnp.broadcast_to(skel_index[:, None, :, No...  313 us
    gather x3, local copies, waits for them, and re-layouts, local(): jnp.take_along_axis(skel_rows, jnp.broadcast_to(skel_index[:, None, None,...  174 us
  transfers between devices with their start and end apart: 7, of which 6 were waited for; matrix products, arithmetic and copies ran while one was open for 2% of the time, Pallas kernels for 0%

commit v1 on v0

--- a/solution.py
+++ b/solution.py
@@ -132,10 +132,10 @@
     from_above = row_recv[:, 3]
     total_blk = own_block.astype(jnp.float32) - (from_left + from_right + from_below + from_above)
     updated = total_blk.astype(jnp.bfloat16)
-    row_shape = (box_count, 2, skel_size, points)
-    total_rows = jnp.take_along_axis(
-        total_blk, jnp.broadcast_to(skel_index[:, None, :, None], row_shape), axis=2
-    )
+    rest = (total_blk - updated.astype(jnp.float32)).astype(jnp.bfloat16)
+    total_rows = jnp.einsum(
+        "bsp,bcpn->bcsn", pick_skel, updated, preferred_element_type=jnp.float32
+    ) + jnp.einsum("bsp,bcpn->bcsn", pick_skel, rest, preferred_element_type=jnp.float32)
     skel_self = select_rows(pick_skel, own_block)
     edge_zero = complex_product("bsp", "brp", "bsr", skel_self, qt_mat).astype(jnp.bfloat16)
     skel_rows = (total_rows - complex_product("bsr", "brn", "bsn", edge_zero, own_factor)).astype(
@@ -149,10 +149,9 @@
         toward_rows.astype(jnp.float32)
         - complex_product("bsr", "brn", "bsn", edge_zero, toward_factor)
     ).astype(jnp.bfloat16)
-    block_shape = (box_count, 2, skel_size, skel_size)
-    skel_block = jnp.take_along_axis(
-        skel_rows, jnp.broadcast_to(skel_index[:, None, None, :], block_shape), axis=3
-    )
+    skel_block = jnp.einsum(
+        "bcsp,btp->bcst", skel_rows, pick_skel, preferred_element_type=jnp.float32
+    ).astype(jnp.bfloat16)
     skel_packed = jnp.concatenate([skel_block[:, 0], skel_block[:, 1]], -1)
     send_pack = jnp.stack([cross_rows[:, 0], cross_rows[:, 1], skel_packed, pick_skel], 1)
     send_half = jnp.where(lower_side, send_pack[half_count:], send_pack[:half_count])

time: 519 us -> 34.7 us (0.07)
  local copies, waits for them, and re-layouts: 490 us -> 5.32 us
    gather x4 -> x0, local copies, waits for them, and re-layouts: 487 us -> none  [the longest x1 313 us: local(): jnp.take_along_axis(total_blk, jnp.broadcast_to(skel_index[:, None, :, No...]
  transfers between devices with their start and end apart: 7 -> 7, of which waited for: 6 -> 5; matrix products, arithmetic and copies ran while one was open for 2% -> 22% of each run, Pallas kernels for 0% -> 0%
where the time goes in v1:
time: 34.7 us; the launch traced here: 34.5 us
  starting transfers between devices  10 us (29%)
  waiting for transfers between devices  8.86 us (26%)
  matrix products  6.11 us (18%)
  local copies, waits for them, and re-layouts  5.32 us (15%)
  other arithmetic  2.82 us (8%)
  between operations  1.42 us (4%)
    ppermute x2, waiting for transfers between devices, padded(): lax.ppermute(tail, axis, [(i, (i + 1) % count) for i in range(count)])  6.73 us
    ppermute x2, starting transfers between devices, padded(): lax.ppermute(head, axis, [((i + 1) % count, i) for i in range(count)])  5.27 us
    unnamed x18, local copies, waits for them, and re-layouts  4.58 us
    dot_general x21, matrix products, complex_product(): return jnp.einsum(form, left_op, mixed, preferred_element_type=jnp.float32)  4.25 us
    ppermute x2, starting transfers between devices, from_behind(): return lax.ppermute(value, axis, pairs)  3.06 us
    ppermute x2, waiting for transfers between devices, padded(): lax.ppermute(head, axis, [((i + 1) % count, i) for i in range(count)])  1.96 us
    ppermute x1, starting transfers between devices, swapped(): return lax.ppermute(value, axis, pairs)  1.45 us
    broadcast_in_dim x1, other arithmetic, local(): coarse = jnp.concatenate([top_rows, bottom_rows], -2)[:, None]  0.73 us
  transfers between devices with their start and end apart: 7, of which 5 were waited for; matrix products, arithmetic and copies ran while one was open for 22% of the time, Pallas kernels for 0%

profile of v1, /device:TPU:0, one launch (start us, length us, event | category | flops | bytes accessed | tf_op | source)
XLA Modules:
  0.0 34.5 jit_solution(1438911064414364334)
XLA Ops:
  0.6 1.1 %copy.312 = bf16[2,1,4,2,128,128]{5,4,3,0,2,1:T(8,128)(2,1)S(1)} copy(bf16[2,1,4,2,128,128]{5,4,3,2,1,0:T(8,128)(2,1)} %param.8) | data formatting | bytes 1048576 | tf_op args[1]
  1.8 0.5 %collective-permute-start.1 = (bf16[2,2,2,128,128]{4,3,2,0,1:T(8,128)(2,1)S(1)}, bf16[2,2,2,128,128]{4,3,2,0,1:T(8,128)(2,1)S(1)}, u32[]{:S(2)}, u32[]{:S(2)}) collective-permute-start(bf16[2,2,2,128,128]{4,3,2,0,1:T(8,128)(2,1)S(1)} %slice.401), channel_id=1, source_target_pairs={{0,1},{1,2},{2,3},{3,0},{4,5},{5,6},{6,7},{7,4},{8,9},{9,10},{10,1... | collective-permute-start | bytes 786440 | tf_op jit(solution)/shard_map/ppermute | solution.py:10
  2.3 2.6 %collective-permute-start = (bf16[1,2,2,128,128]{4,3,2,0,1:T(8,128)(2,1)S(1)}, bf16[1,2,2,128,128]{4,3,2,0,1:T(8,128)(2,1)S(1)}, u32[]{:S(2)}, u32[]{:S(2)}) collective-permute-start(bf16[1,2,2,128,128]{4,3,2,0,1:T(8,128)(2,1)S(1)} %get-tuple-element.30), channel_id=1, source_target_pairs={{0,4},{4,8},{8,12},{12,16},{16,20},{20,24},{24,28},{28,0},{1,5},{5... | collective-permute-start | bytes 393224 | tf_op jit(solution)/shard_map/ppermute | solution.py:10
  4.9 0.3 fusion.164
  5.3 0.7 %copy-done.2 = s32[2,1,64]{2,1,0:T(1,128)S(1)} copy-done((s32[2,1,64]{2,1,0:T(1,128)S(1)}, s32[2,1,64]{2,1,0:T(1,128)}, u32[]{:S(2)}) %copy-start.2) | copy-done | bytes 536
  6.0 0.2 fusion.92
  6.2 0.7 %copy-done.4 = s32[2,1,64]{2,1,0:T(1,128)S(1)} copy-done((s32[2,1,64]{2,1,0:T(1,128)S(1)}, s32[2,1,64]{2,1,0:T(1,128)}, u32[]{:S(2)}) %copy-start.4) | copy-done | bytes 536
  7.4 0.6 %copy-done.1 = bf16[2,1,2,128,128]{4,3,2,1,0:T(8,128)(2,1)S(1)} copy-done((bf16[2,1,2,128,128]{4,3,2,1,0:T(8,128)(2,1)S(1)}, bf16[2,1,2,128,128]{4,3,2,1,0:T(8,128)(2,1)}, u32[]{:S(2)}) %copy-start.1) | copy-done | bytes 131096
  8.0 0.2 fusion.4
  8.5 0.7 %copy-done.5 = s32[2,1,64]{2,1,0:T(1,128)S(1)} copy-done((s32[2,1,64]{2,1,0:T(1,128)S(1)}, s32[2,1,64]{2,1,0:T(1,128)}, u32[]{:S(2)}) %copy-start.5) | copy-done | bytes 536
  9.3 0.2 fusion.58
  10.6 0.2 fusion.54
  11.1 0.2 fusion.50
  12.1 0.2 fusion.56
  12.5 0.2 fusion.34
  12.7 0.2 convolution_bitcast_fusion.2
  13.0 3.6 %collective-permute-start.3 = (bf16[1,2,128,128]{3,2,1,0:T(8,128)(2,1)S(1)}, bf16[1,2,128,128]{3,2,1,0:T(8,128)(2,1)S(1)}, u32[]{:S(2)}, u32[]{:S(2)}) collective-permute-start(bf16[1,2,128,128]{3,2,1,0:T(8,128)(2,1)S(1)} %slice.561), channel_id=1, source_target_pairs={{4,0},{8,4},{12,8},{16,12},{20,16},{24,20},{28,24},{0,28},{5,1},{9... | collective-permute-start | bytes 196616 | tf_op jit(solution)/shard_map/ppermute | solution.py:22
  16.6 0.2 convolution_bitcast_fusion.3
  17.0 1.5 %collective-permute-done.3 = bf16[1,2,128,128]{3,2,1,0:T(8,128)(2,1)S(1)} collective-permute-done((bf16[1,2,128,128]{3,2,1,0:T(8,128)(2,1)S(1)}, bf16[1,2,128,128]{3,2,1,0:T(8,128)(2,1)S(1)}, u32[]{:S(2)}, u32[]{:S(2)}) %collective-permute-start.3) | collective-permute-done | bytes 65568 | tf_op jit(solution)/shard_map/ppermute | solution.py:22
  18.5 5.8 %collective-permute-done.2 = bf16[1,2,128,128]{3,2,1,0:T(8,128)(2,1)S(1)} collective-permute-done((bf16[1,2,128,128]{3,2,1,0:T(8,128)(2,1)S(1)}, bf16[1,2,128,128]{3,2,1,0:T(8,128)(2,1)S(1)}, u32[]{:S(2)}, u32[]{:S(2)}) %collective-permute-start.2) | collective-permute-done | bytes 65568 | tf_op jit(solution)/shard_map/ppermute | solution.py:20
  24.8 0.2 fusion.52
  25.2 0.2 convolution_bitcast_fusion.1
  25.8 0.2 convolution_bitcast_fusion
  26.1 1.7 %collective-permute-start.5 = (bf16[2,1,2,128,128]{4,3,2,0,1:T(8,128)(2,1)S(1)}, bf16[2,1,2,128,128]{4,3,2,0,1:T(8,128)(2,1)S(1)}, u32[]{:S(2)}, u32[]{:S(2)}) collective-permute-start(bf16[2,1,2,128,128]{4,3,2,0,1:T(8,128)(2,1)S(1)} %bitcast.484), channel_id=1, source_target_pairs={{1,0},{2,1},{3,2},{0,3},{5,4},{6,5},{7,6},{4,7},{9,8},{10,9},{11,1... | collective-permute-start | bytes 393224 | tf_op jit(solution)/shard_map/ppermute | solution.py:22
  27.8 0.8 %copy.50 = bf16[2,1,5,2,64,128]{5,4,3,2,1,0:T(8,128)(2,1)} copy(bf16[2,1,5,2,64,128]{5,4,3,0,2,1:T(8,128)(2,1)S(1)} %bitcast.486) | data formatting | bytes 655360
  28.7 0.2 fusion.9
  28.9 0.9 %collective-permute-done.4 = bf16[2,1,2,128,128]{4,3,2,0,1:T(8,128)(2,1)S(1)} collective-permute-done((bf16[2,1,2,128,128]{4,3,2,0,1:T(8,128)(2,1)S(1)}, bf16[2,1,2,128,128]{4,3,2,0,1:T(8,128)(2,1)S(1)}, u32[]{:S(2)}, u32[]{:S(2)}) %collective-permute-start.4) | collective-permute-done | bytes 131104 | tf_op jit(solution)/shard_map/ppermute | solution.py:20
  29.9 0.4 %collective-permute-done.5 = bf16[2,1,2,128,128]{4,3,2,0,1:T(8,128)(2,1)S(1)} collective-permute-done((bf16[2,1,2,128,128]{4,3,2,0,1:T(8,128)(2,1)S(1)}, bf16[2,1,2,128,128]{4,3,2,0,1:T(8,128)(2,1)S(1)}, u32[]{:S(2)}, u32[]{:S(2)}) %collective-permute-start.5) | collective-permute-done | bytes 131104 | tf_op jit(solution)/shard_map/ppermute | solution.py:22
  30.6 0.3 convolution_convert_fusion
  31.1 1.5 %collective-permute-start.6 = (bf16[1,4,64,128]{3,2,1,0:T(8,128)(2,1)S(1)}, bf16[1,4,64,128]{3,2,1,0:T(8,128)(2,1)S(1)}, u32[]{:S(2)}, u32[]{:S(2)}) collective-permute-start(bf16[1,4,64,128]{3,2,1,0:T(8,128)(2,1)S(1)} %slice_select_fusion), channel_id=1, source_target_pairs={{0,1},{1,0},{2,3},{3,2},{4,5},{5,4},{6,7},{7,6},{8,9},{9,8},{10,11... | collective-permute-start | bytes 196616 | tf_op jit(solution)/shard_map/ppermute | solution.py:32
  32.5 0.7 %fusion.63 = bf16[2,1,2,128,128]{4,3,2,1,0:T(8,128)(2,1)} fusion(bf16[2,1,2,128,128]{4,3,2,0,1:T(8,128)(2,1)S(1)} %get-tuple-element.11, bf16[2,1,2,128,128]{4,3,2,0,1:T(8,128)(2,1)S(1)} %get-tuple-element.10, f32[1,1,2,128,128]{4,3,2,1,0:T(8,128)S(1)} %bitcast.475, f32[1,1,2,128,128]{4,3,2,1,0:T(8,128)S(1)} %get-tuple-element.34, ...), kind=kLoop, calls=%fused_computation.140 | loop fusion | flops 655360 | bytes 1048576
  33.8 0.7 %maximum_bitcast_fusion.21 = bf16[1,1,2,128,128]{4,3,2,1,0:T(8,128)(2,1)} fusion(bf16[1,2,64,64]{3,2,1,0:T(8,128)(2,1)S(1)} %get-tuple-element.66, bf16[1,2,64,64]{3,2,1,0:T(8,128)(2,1)S(1)} %get-tuple-element.68, bf16[1,2,64,64]{3,2,1,0:T(8,128)(2,1)S(1)} %get-tuple-element.67, bf16[1,2,64,64]{3,2,1,0:T(8,128)(2,1)S(1)} %get-tuple-element.65), kind=kLoop, calls=%fused_computation.179 | loop fusion | flops 262144 | bytes 131072 | tf_op jit(solution)/shard_map/broadcast_in_dim | solution.py:177
  (113 shorter events, 5.3 us)
Async XLA Ops:
  0.6 7.8 %copy-start = (bf16[2,1,2,64,64]{4,3,2,1,0:T(8,128)(2,1)S(1)}, bf16[2,1,2,64,64]{4,3,2,1,0:T(8,128)(2,1)}, u32[]{:S(2)}) copy-start(bf16[2,1,2,64,64]{4,3,2,1,0:T(8,128)(2,1)} %param.13) | copy-start | bytes 98308
  1.8 22.6 %collective-permute-start.1 = (bf16[2,2,2,128,128]{4,3,2,0,1:T(8,128)(2,1)S(1)}, bf16[2,2,2,128,128]{4,3,2,0,1:T(8,128)(2,1)S(1)}, u32[]{:S(2)}, u32[]{:S(2)}) collective-permute-start(bf16[2,2,2,128,128]{4,3,2,0,1:T(8,128)(2,1)S(1)} %slice.401), channel_id=1, source_target_pairs={{0,1},{1,2},{2,3},{3,0},{4,5},{5,6},{6,7},{7,4},{8,9},{9,10},{10,1... | collective-permute-start | bytes 786440 | tf_op jit(solution)/shard_map/ppermute | solution.py:10
  2.3 2.8 %copy-start.3 = (bf16[2,1,2,64,64]{4,3,2,1,0:T(8,128)(2,1)S(1)}, bf16[2,1,2,64,64]{4,3,2,1,0:T(8,128)(2,1)}, u32[]{:S(2)}) copy-start(bf16[2,1,2,64,64]{4,3,2,1,0:T(8,128)(2,1)} %param.11) | copy-start | bytes 98308
  2.3 9.5 %collective-permute-start = (bf16[1,2,2,128,128]{4,3,2,0,1:T(8,128)(2,1)S(1)}, bf16[1,2,2,128,128]{4,3,2,0,1:T(8,128)(2,1)S(1)}, u32[]{:S(2)}, u32[]{:S(2)}) collective-permute-start(bf16[1,2,2,128,128]{4,3,2,0,1:T(8,128)(2,1)S(1)} %get-tuple-element.30), channel_id=1, source_target_pairs={{0,4},{4,8},{8,12},{12,16},{16,20},{20,24},{24,28},{28,0},{1,5},{5... | collective-permute-start | bytes 393224 | tf_op jit(solution)/shard_map/ppermute | solution.py:10
  5.3 0.7 %copy-start.2 = (s32[2,1,64]{2,1,0:T(1,128)S(1)}, s32[2,1,64]{2,1,0:T(1,128)}, u32[]{:S(2)}) copy-start(s32[2,1,64]{2,1,0:T(1,128)} %param.9) | copy-start | bytes 1540
  6.2 0.7 %copy-start.4 = (s32[2,1,64]{2,1,0:T(1,128)S(1)}, s32[2,1,64]{2,1,0:T(1,128)}, u32[]{:S(2)}) copy-start(s32[2,1,64]{2,1,0:T(1,128)} %param.10) | copy-start | bytes 1540
  7.1 0.9 %copy-start.1 = (bf16[2,1,2,128,128]{4,3,2,1,0:T(8,128)(2,1)S(1)}, bf16[2,1,2,128,128]{4,3,2,1,0:T(8,128)(2,1)}, u32[]{:S(2)}) copy-start(bf16[2,1,2,128,128]{4,3,2,1,0:T(8,128)(2,1)} %param.7) | copy-start | bytes 393220
  8.4 0.7 %copy-start.5 = (s32[2,1,64]{2,1,0:T(1,128)S(1)}, s32[2,1,64]{2,1,0:T(1,128)}, u32[]{:S(2)}) copy-start(s32[2,1,64]{2,1,0:T(1,128)} %param.12) | copy-start | bytes 1540
  13.0 5.5 %collective-permute-start.3 = (bf16[1,2,128,128]{3,2,1,0:T(8,128)(2,1)S(1)}, bf16[1,2,128,128]{3,2,1,0:T(8,128)(2,1)S(1)}, u32[]{:S(2)}, u32[]{:S(2)}) collective-permute-start(bf16[1,2,128,128]{3,2,1,0:T(8,128)(2,1)S(1)} %slice.561), channel_id=1, source_target_pairs={{4,0},{8,4},{12,8},{16,12},{20,16},{24,20},{28,24},{0,28},{5,1},{9... | collective-permute-start | bytes 196616 | tf_op jit(solution)/shard_map/ppermute | solution.py:22
  16.9 7.4 %collective-permute-start.2 = (bf16[1,2,128,128]{3,2,1,0:T(8,128)(2,1)S(1)}, bf16[1,2,128,128]{3,2,1,0:T(8,128)(2,1)S(1)}, u32[]{:S(2)}, u32[]{:S(2)}) collective-permute-start(bf16[1,2,128,128]{3,2,1,0:T(8,128)(2,1)S(1)} %slice.562), channel_id=1, source_target_pairs={{0,4},{4,8},{8,12},{12,16},{16,20},{20,24},{24,28},{28,0},{1,5},{5... | collective-permute-start | bytes 196616 | tf_op jit(solution)/shard_map/ppermute | solution.py:20
  25.4 4.4 %collective-permute-start.4 = (bf16[2,1,2,128,128]{4,3,2,0,1:T(8,128)(2,1)S(1)}, bf16[2,1,2,128,128]{4,3,2,0,1:T(8,128)(2,1)S(1)}, u32[]{:S(2)}, u32[]{:S(2)}) collective-permute-start(bf16[2,1,2,128,128]{4,3,2,0,1:T(8,128)(2,1)S(1)} %bitcast.482), channel_id=1, source_target_pairs={{0,1},{1,2},{2,3},{3,0},{4,5},{5,6},{6,7},{7,4},{8,9},{9,10},{10,1... | collective-permute-start | bytes 393224 | tf_op jit(solution)/shard_map/ppermute | solution.py:20
  26.1 4.2 %collective-permute-start.5 = (bf16[2,1,2,128,128]{4,3,2,0,1:T(8,128)(2,1)S(1)}, bf16[2,1,2,128,128]{4,3,2,0,1:T(8,128)(2,1)S(1)}, u32[]{:S(2)}, u32[]{:S(2)}) collective-permute-start(bf16[2,1,2,128,128]{4,3,2,0,1:T(8,128)(2,1)S(1)} %bitcast.484), channel_id=1, source_target_pairs={{1,0},{2,1},{3,2},{0,3},{5,4},{6,5},{7,6},{4,7},{9,8},{10,9},{11,1... | collective-permute-start | bytes 393224 | tf_op jit(solution)/shard_map/ppermute | solution.py:22
  31.1 2.4 %collective-permute-start.6 = (bf16[1,4,64,128]{3,2,1,0:T(8,128)(2,1)S(1)}, bf16[1,4,64,128]{3,2,1,0:T(8,128)(2,1)S(1)}, u32[]{:S(2)}, u32[]{:S(2)}) collective-permute-start(bf16[1,4,64,128]{3,2,1,0:T(8,128)(2,1)S(1)} %slice_select_fusion), channel_id=1, source_target_pairs={{0,1},{1,0},{2,3},{3,2},{4,5},{5,4},{6,7},{7,6},{8,9},{9,8},{10,11... | collective-permute-start | bytes 196616 | tf_op jit(solution)/shard_map/ppermute | solution.py:32

commit v2 on v1

v2 whole, which is shorter than its diff:
```python
import jax
import jax.numpy as jnp
from jax import lax
from jax.experimental import pallas as pl
from jax.experimental.pallas import tpu as pltpu
from jax.sharding import PartitionSpec as P

MESH = pl.DeviceIdType.MESH
BF16, F32 = jnp.bfloat16, jnp.float32


def dot(left_op, right_op):
    return jnp.dot(left_op, right_op, preferred_element_type=F32)


def dot_nt(left_op, right_op):
    return lax.dot_general(left_op, right_op, (((1,), (1,)), ((), ())), preferred_element_type=F32)


def cat(axis, *parts):
    return jnp.concatenate(parts, axis)


def beside(ref, *index):
    return cat(1, ref[(*index, 0)], ref[(*index, 1)])


def above(ref, *index):
    return cat(0, ref[(*index, 0)], ref[(*index, 1)])


def folded(wide):
    half = wide.shape[1] // 2
    return cat(0, wide[:, :half], wide[:, half:])


def paired(tall):
    half = tall.shape[0] // 2
    return cat(1, tall[:half], tall[half:])


def make_params(par, pick, skel, red, interp, pivot, inverse, j):
    points, size = pick.shape[2], skel.shape[2]
    ids = lax.broadcasted_iota(jnp.int32, (points, size), 0)
    skel_t = jnp.where(ids == skel[j], 1.0, 0.0)
    red_t = jnp.where(ids == red[j], 1.0, 0.0)
    order = jnp.where(ids[:size] == pivot[j], 1.0, 0.0).astype(BF16)
    spread = dot(skel_t.astype(BF16), beside(interp, j))
    q_t = cat(1, red_t, jnp.zeros_like(red_t)) - spread
    par[j, 0 : 2 * size, :] = q_t.T.astype(BF16)
    turned = dot_nt(above(inverse, j), order).astype(BF16)
    par[j, 2 * size : 3 * size, :] = paired(turned)
    pick[j] = cat(1, skel_t, red_t).T[:size].astype(BF16)


def read_params(block):
    size = block.shape[0] // 3
    q_re, q_im, inv = block[:size], block[size : 2 * size], block[2 * size :]
    real_row, imag_row = cat(1, q_re, -q_im), cat(1, q_im, q_re)
    q_mix = cat(0, real_row, imag_row)
    e_mix = cat(0, real_row, -imag_row, imag_row, real_row)
    inv_re, inv_im = inv[:, :size], inv[:, size:]
    inv_mix = cat(0, cat(1, inv_re, -inv_im), cat(1, inv_im, inv_re))
    return q_mix, e_mix, inv_mix


def factors(params, right_op):
    q_mix, _, inv_mix = params
    return dot(inv_mix, dot(q_mix, right_op).astype(BF16)).astype(BF16)


def kernel(
    self_hbm, coup_hbm, skel_hbm, red_hbm, interp_hbm, pivot_hbm, inverse_hbm,
    factor_out, updated_out, coarse_out,
    own, coup, skel, red, interp, pivot, inverse,
    pick, par, par_x, par_y, extra, extra_y, fac, acc, w_send_x, w_send_y, w_x, w_y,
    self_term, keep_k, g_own, g_other, updated, coarse,
    in_sem, send_sem, recv_sem, out_sem,
):
    n, points = own.shape[0], own.shape[2]
    half, size = n // 2, skel.shape[2]
    gx, gy = lax.axis_index("gx"), lax.axis_index("gy")
    nx, ny = lax.axis_size("gx"), lax.axis_size("gy")
    x_next, x_back = {"gx": lax.rem(gx + 1, nx)}, {"gx": lax.rem(gx + nx - 1, nx)}
    y_next, y_back = {"gy": lax.rem(gy + 1, ny)}, {"gy": lax.rem(gy + ny - 1, ny)}
    odd = lax.rem(gy, 2)
    partner = {"gy": gy + 1 - 2 * odd}

    barrier = pltpu.get_barrier_semaphore()
    for device in (x_next, x_back, y_next, y_back):
        pl.semaphore_signal(barrier, inc=1, device_id=device, device_id_type=MESH)

    def load(source, target, at):
        copy = pltpu.make_async_copy(source, target, in_sem.at[at])
        copy.start()
        return copy

    small = [
        load(skel_hbm, skel, 0),
        load(red_hbm, red, 1),
        load(interp_hbm.at[:, 0], interp, 2),
        load(pivot_hbm, pivot, 3),
        load(inverse_hbm.at[:, 0], inverse, 4),
    ]
    large = []
    for j in range(n):
        large.append(
            (
                load(coup_hbm.at[j, 0], coup.at[j], 5 + 2 * j),
                load(self_hbm.at[j, 0], own.at[j], 6 + 2 * j),
            )
        )

    def remote(source, target, at, device):
        return pltpu.make_async_remote_copy(
            src_ref=source, dst_ref=target, send_sem=send_sem.at[at],
            recv_sem=recv_sem.at[at], device_id=device, device_id_type=MESH,
        )

    outs = []

    def store(source, target):
        copy = pltpu.make_async_copy(source, target, out_sem.at[len(outs)])
        copy.start()
        outs.append(copy)

    send_par_x = remote(par.at[0], par_x, 0, x_back)
    send_par_y = remote(par, par_y, 1, y_back)
    send_extra = remote(extra, extra_y, 2, y_back)
    send_w_x = remote(w_send_x, w_x, 3, x_next)
    send_k = remote(keep_k.at[pl.ds(half, half)], keep_k.at[pl.ds(0, half)], 4, partner)
    send_g = remote(g_own.at[pl.ds((1 - odd) * half, half)], g_other, 5, partner)
    send_fac_x = remote(fac.at[n - 1, 1], factor_out.at[0, 0, 1], 6, x_next)
    send_w_y = [remote(w_send_y.at[j], w_y.at[j], 7 + 2 * j, y_next) for j in range(n)]
    send_fac_y = [
        remote(fac.at[j, 3], factor_out.at[j, 0, 3], 8 + 2 * j, y_next) for j in range(n)
    ]

    def put_factor(j, k, value):
        fac[j, k] = value.reshape(2, size, points)

    for copy in small:
        copy.wait()
    for j in range(n):
        make_params(par, pick, skel, red, interp, pivot, inverse, j)
    pl.semaphore_wait(barrier, 4)
    send_par_y.start()
    send_par_x.start()

    for j in range(n):
        for copy in large[j]:
            copy.wait()
    params = [read_params(par[j]) for j in range(n)]
    w_right = []
    for j in range(n):
        right_ops = cat(1, above(coup, j, 2), above(coup, j, 0), above(own, j))
        made = factors(params[j], right_ops)
        f_up, f_right, f_own = (made[:, k * points : (k + 1) * points] for k in range(3))
        put_factor(j, 4, f_up)
        put_factor(j, 2, f_right)
        put_factor(j, 0, f_own)
        own_rows = dot(pick[j], beside(own, j)).astype(BF16)
        left_ops = cat(0, beside(coup, j, 3), beside(coup, j, 1), own_rows)
        ends = dot_nt(left_ops, params[j][1]).astype(BF16)
        w_send_y[j] = dot(folded(ends[:points]), f_up).astype(BF16)
        send_w_y[j].start()
        w_right.append(dot(folded(ends[points : 2 * points]), f_right))
        if j == n - 1:
            w_send_x[...] = w_right[j].astype(BF16)
            send_w_x.start()
        e_mix = folded(ends[2 * points :])
        self_term[j] = dot(e_mix, cat(1, f_own, f_up))
        extra[j, :size, :] = cat(1, e_mix[:size, :size], e_mix[size:, :size])
        extra[j, size:, :] = pick[j]
        acc[j] = above(own, j).astype(F32)
        if j > 0:
            acc[j] = acc[j] - w_right[j - 1]

    @pl.when(odd == 1)
    def _():
        send_extra.start()

    for j in range(n):
        for k in (0, 2, 4):
            store(fac.at[j, k], factor_out.at[j, 0, k])

    def from_next(next_params, j, k):
        made = factors(next_params, above(coup, j, k))
        put_factor(j, k, made)
        ends = dot_nt(beside(coup, j, k - 1), next_params[1]).astype(BF16)
        return made, dot(folded(ends), made)

    for j in range(n - 1):
        acc[j] = acc[j] - from_next(params[j + 1], j, 1)[1]
        store(fac.at[j, 1], factor_out.at[j + 1, 0, 1])
    send_par_y.wait_recv()
    for j in range(n):
        acc[j] = acc[j] - from_next(read_params(par_y[j]), j, 3)[1]
        send_fac_y[j].start()
    send_par_x.wait_recv()
    acc[n - 1] = acc[n - 1] - from_next(read_params(par_x[...]), n - 1, 1)[1]
    send_fac_x.start()

    @pl.when(odd == 0)
    def _():
        send_extra.wait_recv()
        for j in reversed(range(n)):
            lower_pick, upper_pick = pick[j], extra_y[j, size:, :]
            rows = folded(dot(lower_pick, beside(coup, j, 2))) - self_term[j, :, points:]
            keep_k[j, 0] = paired(dot_nt(rows.astype(BF16), upper_pick).astype(BF16))
            end = extra_y[j, :size, :]
            e_re, e_im = end[:, :size], end[:, size:]
            e_mix = cat(0, cat(1, e_re, -e_im), cat(1, e_im, e_re))
            upper_factor = above(fac, j, 3)
            rows = folded(dot(upper_pick, beside(coup, j, 3))) - dot(e_mix, upper_factor)
            keep_k[j, 1] = paired(dot_nt(rows.astype(BF16), lower_pick).astype(BF16))
        send_k.start()

    send_w_x.wait_recv()
    for j in range(n):
        send_w_y[j].wait_recv()
    for j in range(n):
        total = acc[j] - w_y[j].astype(F32)
        if j == 0:
            total = total - w_x[...].astype(F32)
        rounded = total.astype(BF16)
        rest = (total - rounded.astype(F32)).astype(BF16)
        updated[j] = rounded.reshape(2, points, points)
        rows = dot(pick[j], cat(1, paired(rounded), paired(rest)))
        rows = rows[:, : 2 * points] + rows[:, 2 * points :]
        rows = (folded(rows) - self_term[j, :, :points]).astype(BF16)
        g_own[j] = paired(dot_nt(rows, pick[j]).astype(BF16))
    send_g.start()
    for j in range(n):
        store(updated.at[j], updated_out.at[j, 0])

    @pl.when(odd == 1)
    def _():
        send_k.wait_recv()

    send_g.wait_recv()
    for t in range(half):
        mine, other = g_own[odd * half + t], g_other[t]
        lower = jnp.where(odd == 0, mine, other)
        upper = jnp.where(odd == 0, other, mine)
        k_lower, k_upper = keep_k[t, 0], keep_k[t, 1]
        for c in range(2):
            part = slice(c * size, (c + 1) * size)
            coarse[t, c, :size, :] = cat(1, lower[:, part], k_lower[:, part])
            coarse[t, c, size:, :] = cat(1, k_upper[:, part], upper[:, part])
    store(coarse, coarse_out.at[:, 0])

    send_fac_x.wait_recv()
    for copy in send_fac_y:
        copy.wait_recv()
    for copy in [send_par_x, send_par_y, send_w_x, send_g, send_fac_x, *send_w_y, *send_fac_y]:
        copy.wait_send()

    @pl.when(odd == 1)
    def _():
        send_extra.wait_send()

    @pl.when(odd == 0)
    def _():
        send_k.wait_send()

    for copy in outs:
        copy.wait()


def local(self_block, coupling, skeleton, redundant, interp, pivot, pivot_inverse):
    n, _, _, points, _ = self_block.shape
    size, half = skeleton.shape[2], n // 2
    vmem = pltpu.VMEM
    return pl.pallas_call(
        kernel,
        out_shape=(
            jax.ShapeDtypeStruct((n, 1, 5, 2, size, points), BF16),
            jax.ShapeDtypeStruct((n, 1, 2, points, points), BF16),
            jax.ShapeDtypeStruct((half, 1, 2, points, points), BF16),
        ),
        in_specs=[pl.BlockSpec(memory_space=pl.ANY)] * 7,
        out_specs=(pl.BlockSpec(memory_space=pl.ANY),) * 3,
        scratch_shapes=[
            vmem((n, 2, points, points), BF16),
            vmem((n, 4, 2, points, points), BF16),
            vmem((n, 1, size), jnp.int32),
            vmem((n, 1, size), jnp.int32),
            vmem((n, 2, size, size), BF16),
            vmem((n, 1, size), jnp.int32),
            vmem((n, 2, size, size), BF16),
            vmem((n, size, points), BF16),
            vmem((n, 3 * size, points), BF16),
            vmem((3 * size, points), BF16),
            vmem((n, 3 * size, points), BF16),
            vmem((n, 2 * size, points), BF16),
            vmem((n, 2 * size, points), BF16),
            vmem((n, 5, 2, size, points), BF16),
            vmem((n, 2 * points, points), F32),
            vmem((2 * points, points), BF16),
            vmem((n, 2 * points, points), BF16),
            vmem((2 * points, points), BF16),
            vmem((n, 2 * points, points), BF16),
            vmem((n, 2 * size, 2 * points), F32),
            vmem((n, 2, size, 2 * size), BF16),
            vmem((n, size, 2 * size), BF16),
            vmem((half, size, 2 * size), BF16),
            vmem((n, 2, points, points), BF16),
            vmem((half, 2, points, points), BF16),
            pltpu.SemaphoreType.DMA((5 + 2 * n,)),
            pltpu.SemaphoreType.DMA((7 + 2 * n,)),
            pltpu.SemaphoreType.DMA((7 + 2 * n,)),
            pltpu.SemaphoreType.DMA((5 * n,)),
        ],
        compiler_params=pltpu.CompilerParams(
            collective_id=0, has_side_effects=True, vmem_limit_bytes=24 * 2**20
        ),
    )(self_block, coupling, skeleton, redundant, interp, pivot, pivot_inverse)


def solution(mesh):
    box = P("gx", "gy", None, None, None)
    wide = P("gx", "gy", None, None, None, None)
    index = P("gx", "gy", None)
    return jax.shard_map(
        local,
        mesh=mesh,
        in_specs=(box, wide, index, index, box, index, box),
        out_specs=(wide, box, box),
        check_vma=False,
    )
```

time: 34.7 us -> 24.1 us (0.69)
  Pallas kernels: 0 us -> 15.5 us
  starting transfers between devices: 10 us -> 0 us
  waiting for transfers between devices: 8.86 us -> 0 us
  matrix products: 6.11 us -> 0 us
  other arithmetic: 2.82 us -> 0 us
  local copies, waits for them, and re-layouts: 5.32 us -> 7.66 us
  between operations: 1.42 us -> 0.66 us
    pallas_call x0 -> x1, Pallas kernels: none -> 15.5 us  [local(): pl.pallas_call(kernel, out_shape=(jax.ShapeDtypeStruct((n, 1, 5, 2, size,...]
    ppermute x7 -> x0, starting transfers between devices: 10 us -> none  [the longest x2 5.27 us: padded(): lax.ppermute(head, axis, [((i + 1) % count, i) for i in range(count)])]
    ppermute x7 -> x0, waiting for transfers between devices: 8.86 us -> none  [the longest x2 6.73 us: padded(): lax.ppermute(tail, axis, [(i, (i + 1) % count) for i in range(count)])]
    dot_general x29 -> x0, matrix products: 5.89 us -> none  [the longest x21 4.25 us: complex_product(): return jnp.einsum(form, left_op, mixed, preferred_element_type=jnp.float32)]
    unnamed x18 -> x17, local copies, waits for them, and re-layouts: 4.58 us -> 7.66 us
    broadcast_in_dim x1 -> x0, other arithmetic: 0.73 us -> none  [local(): coarse = jnp.concatenate([top_rows, bottom_rows], -2)[:, None]]
    unnamed x1 -> x0, other arithmetic: 0.73 us -> none
    another operation x28 -> x0, other arithmetic: 0.59 us -> none  [the longest x24 0.39 us: complex_product(): jnp.stack([jnp.stack([right_op[:, 0], right_op[:, 1]], 1), jnp.stack([-ri...]
  transfers between devices with their start and end apart: 7 -> 0, of which waited for: 5 -> 0; matrix products, arithmetic and copies ran while one was open for 22% -> 0% of each run, Pallas kernels for 0% -> 0%
where the time goes in v2:
time: 24.1 us; the launch traced here: 23.8 us
  Pallas kernels  15.5 us (64%)
  local copies, waits for them, and re-layouts  7.66 us (32%)
  between operations  0.66 us (3%)
    pallas_call x1, Pallas kernels, local(): pl.pallas_call(kernel, out_shape=(jax.ShapeDtypeStruct((n, 1, 5, 2, size,...  15.5 us
    unnamed x17, local copies, waits for them, and re-layouts  7.66 us

profile of v2, /device:TPU:0, one launch (start us, length us, event | category | flops | bytes accessed | tf_op | source)
XLA Modules:
  0.0 23.8 jit_solution(16017041499158636321)
XLA Ops:
  0.6 0.0 copy-start
  0.6 1.0 %copy-done = bf16[2,1,4,2,128,128]{5,4,3,2,1,0:T(8,128)(2,1)S(1)} copy-done((bf16[2,1,4,2,128,128]{5,4,3,2,1,0:T(8,128)(2,1)S(1)}, bf16[2,1,4,2,128,128]{5,4,3,2,1,0:T(8,128)(2,1)}, u32[]{:S(2)}) %copy-start) | copy-done | bytes 524312
  1.7 0.0 copy-start.1
  1.7 0.9 %copy-done.1 = bf16[2,1,2,128,128]{4,3,2,1,0:T(8,128)(2,1)S(1)} copy-done((bf16[2,1,2,128,128]{4,3,2,1,0:T(8,128)(2,1)S(1)}, bf16[2,1,2,128,128]{4,3,2,1,0:T(8,128)(2,1)}, u32[]{:S(2)}) %copy-start.1) | copy-done | bytes 131096
  2.6 0.0 copy-start.2
  2.6 0.8 %copy-done.2 = bf16[2,1,2,64,64]{4,3,2,1,0:T(8,128)(2,1)S(1)} copy-done((bf16[2,1,2,64,64]{4,3,2,1,0:T(8,128)(2,1)S(1)}, bf16[2,1,2,64,64]{4,3,2,1,0:T(8,128)(2,1)}, u32[]{:S(2)}) %copy-start.2) | copy-done | bytes 32792
  3.4 0.0 copy-start.3
  3.4 0.8 %copy-done.3 = bf16[2,1,2,64,64]{4,3,2,1,0:T(8,128)(2,1)S(1)} copy-done((bf16[2,1,2,64,64]{4,3,2,1,0:T(8,128)(2,1)S(1)}, bf16[2,1,2,64,64]{4,3,2,1,0:T(8,128)(2,1)}, u32[]{:S(2)}) %copy-start.3) | copy-done | bytes 32792
  4.3 0.0 copy-start.4
  4.3 0.7 %copy-done.4 = s32[2,1,64]{2,1,0:T(1,128)S(1)} copy-done((s32[2,1,64]{2,1,0:T(1,128)S(1)}, s32[2,1,64]{2,1,0:T(1,128)}, u32[]{:S(2)}) %copy-start.4) | copy-done | bytes 536
  4.9 0.0 copy-start.5
  4.9 0.7 %copy-done.5 = s32[2,1,64]{2,1,0:T(1,128)S(1)} copy-done((s32[2,1,64]{2,1,0:T(1,128)S(1)}, s32[2,1,64]{2,1,0:T(1,128)}, u32[]{:S(2)}) %copy-start.5) | copy-done | bytes 536
  5.6 0.0 copy-start.6
  5.6 0.7 %copy-done.6 = s32[2,1,64]{2,1,0:T(1,128)S(1)} copy-done((s32[2,1,64]{2,1,0:T(1,128)S(1)}, s32[2,1,64]{2,1,0:T(1,128)}, u32[]{:S(2)}) %copy-start.6) | copy-done | bytes 536
  6.3 15.5 %shard_map.94 = (bf16[2,1,5,2,64,128]{5,4,3,2,1,0:T(8,128)(2,1)S(1)}, bf16[2,1,2,128,128]{4,3,2,1,0:T(8,128)(2,1)S(1)}, bf16[1,1,2,128,128]{4,3,2,1,0:T(8,128)(2,1)S(1)}) custom-call(bf16[2,1,2,128,128]{4,3,2,1,0:T(8,128)(2,1)S(1)} %copy-done.1, bf16[2,1,4,2,128,128]{5,4,3,2,1,0:T(8,128)(2,1)S(1)} %copy-done, s32[2,1,64]{2,1,0:T(1,128)S(1)} %copy-done.4, ...), custom_call_target="tpu_custom_call" | custom-call | tf_op jit(solution)/shard_map/pallas_call | solution.py:275
  21.8 0.7 %copy.13 = bf16[2,1,5,2,64,128]{5,4,3,2,1,0:T(8,128)(2,1)} copy(bf16[2,1,5,2,64,128]{5,4,3,2,1,0:T(8,128)(2,1)S(1)} %get-tuple-element.6) | data formatting | bytes 655360
  22.5 0.7 %copy.14 = bf16[2,1,2,128,128]{4,3,2,1,0:T(8,128)(2,1)} copy(bf16[2,1,2,128,128]{4,3,2,1,0:T(8,128)(2,1)S(1)} %get-tuple-element.7) | data formatting | bytes 262144
  23.2 0.6 %copy.15 = bf16[1,1,2,128,128]{4,3,2,1,0:T(8,128)(2,1)} copy(bf16[1,1,2,128,128]{4,3,2,1,0:T(8,128)(2,1)S(1)} %get-tuple-element.8) | data formatting | bytes 131072
Async XLA Ops:
  0.6 1.0 %copy-start = (bf16[2,1,4,2,128,128]{5,4,3,2,1,0:T(8,128)(2,1)S(1)}, bf16[2,1,4,2,128,128]{5,4,3,2,1,0:T(8,128)(2,1)}, u32[]{:S(2)}) copy-start(bf16[2,1,4,2,128,128]{5,4,3,2,1,0:T(8,128)(2,1)} %coup_hbm.1) | copy-start | bytes 1572868
  1.7 0.9 %copy-start.1 = (bf16[2,1,2,128,128]{4,3,2,1,0:T(8,128)(2,1)S(1)}, bf16[2,1,2,128,128]{4,3,2,1,0:T(8,128)(2,1)}, u32[]{:S(2)}) copy-start(bf16[2,1,2,128,128]{4,3,2,1,0:T(8,128)(2,1)} %self_hbm.1) | copy-start | bytes 393220
  2.6 0.8 %copy-start.2 = (bf16[2,1,2,64,64]{4,3,2,1,0:T(8,128)(2,1)S(1)}, bf16[2,1,2,64,64]{4,3,2,1,0:T(8,128)(2,1)}, u32[]{:S(2)}) copy-start(bf16[2,1,2,64,64]{4,3,2,1,0:T(8,128)(2,1)} %interp_hbm.1) | copy-start | bytes 98308
  3.4 0.8 %copy-start.3 = (bf16[2,1,2,64,64]{4,3,2,1,0:T(8,128)(2,1)S(1)}, bf16[2,1,2,64,64]{4,3,2,1,0:T(8,128)(2,1)}, u32[]{:S(2)}) copy-start(bf16[2,1,2,64,64]{4,3,2,1,0:T(8,128)(2,1)} %inverse_hbm.1) | copy-start | bytes 98308
  4.3 0.7 %copy-start.4 = (s32[2,1,64]{2,1,0:T(1,128)S(1)}, s32[2,1,64]{2,1,0:T(1,128)}, u32[]{:S(2)}) copy-start(s32[2,1,64]{2,1,0:T(1,128)} %skel_hbm.1) | copy-start | bytes 1540
  4.9 0.7 %copy-start.5 = (s32[2,1,64]{2,1,0:T(1,128)S(1)}, s32[2,1,64]{2,1,0:T(1,128)}, u32[]{:S(2)}) copy-start(s32[2,1,64]{2,1,0:T(1,128)} %red_hbm.1) | copy-start | bytes 1540
  5.6 0.7 %copy-start.6 = (s32[2,1,64]{2,1,0:T(1,128)S(1)}, s32[2,1,64]{2,1,0:T(1,128)}, u32[]{:S(2)}) copy-start(s32[2,1,64]{2,1,0:T(1,128)} %pivot_hbm.1) | copy-start | bytes 1540

commit v3 on v2

--- a/solution.py
+++ b/solution.py
@@ -268,17 +268,30 @@
         copy.wait()
 
 
+def hand_over(*refs):
+    sources, targets, sem = refs[:3], refs[3:6], refs[6]
+    copies = [
+        pltpu.make_async_copy(source, target, sem.at[at])
+        for at, (source, target) in enumerate(zip(sources, targets))
+    ]
+    for copy in copies:
+        copy.start()
+    for copy in copies:
+        copy.wait()
+
+
 def local(self_block, coupling, skeleton, redundant, interp, pivot, pivot_inverse):
     n, _, _, points, _ = self_block.shape
     size, half = skeleton.shape[2], n // 2
     vmem = pltpu.VMEM
-    return pl.pallas_call(
+    shapes = (
+        jax.ShapeDtypeStruct((n, 1, 5, 2, size, points), BF16),
+        jax.ShapeDtypeStruct((n, 1, 2, points, points), BF16),
+        jax.ShapeDtypeStruct((half, 1, 2, points, points), BF16),
+    )
+    made = pl.pallas_call(
         kernel,
-        out_shape=(
-            jax.ShapeDtypeStruct((n, 1, 5, 2, size, points), BF16),
-            jax.ShapeDtypeStruct((n, 1, 2, points, points), BF16),
-            jax.ShapeDtypeStruct((half, 1, 2, points, points), BF16),
-        ),
+        out_shape=shapes,
         in_specs=[pl.BlockSpec(memory_space=pl.ANY)] * 7,
         out_specs=(pl.BlockSpec(memory_space=pl.ANY),) * 3,
         scratch_shapes=[
@@ -313,9 +326,17 @@
             pltpu.SemaphoreType.DMA((5 * n,)),
         ],
         compiler_params=pltpu.CompilerParams(
-            collective_id=0, has_side_effects=True, vmem_limit_bytes=24 * 2**20
+            collective_id=0, has_side_effects=True, vmem_limit_bytes=62 * 2**20
         ),
     )(self_block, coupling, skeleton, redundant, interp, pivot, pivot_inverse)
+    return pl.pallas_call(
+        hand_over,
+        out_shape=shapes,
+        in_specs=[pl.BlockSpec(memory_space=pl.ANY)] * 3,
+        out_specs=(pl.BlockSpec(memory_space=pltpu.HBM),) * 3,
+        scratch_shapes=[pltpu.SemaphoreType.DMA((3,))],
+        compiler_params=pltpu.CompilerParams(vmem_limit_bytes=62 * 2**20),
+    )(*made)
 
 
 def solution(mesh):

time: 24.1 us -> 33.8 us (1.40)
  Pallas kernels: 15.5 us -> 33 us
  local copies, waits for them, and re-layouts: 7.66 us -> 0 us
    pallas_call x1 -> x2, Pallas kernels: 15.5 us -> 33 us  [the longest x1 17 us: local(): pl.pallas_call(hand_over, out_shape=shapes, in_specs=[pl.BlockSpec(memory...]
    unnamed x17 -> x0, local copies, waits for them, and re-layouts: 7.66 us -> none
where the time goes in v3:
time: 33.8 us; the launch traced here: 33.6 us
  Pallas kernels  33 us (98%)
  between operations  0.64 us (2%)
    pallas_call x1, Pallas kernels, local(): pl.pallas_call(hand_over, out_shape=shapes, in_specs=[pl.BlockSpec(memory...  17 us
    pallas_call x1, Pallas kernels, local(): pl.pallas_call(kernel, out_shape=shapes, in_specs=[pl.BlockSpec(memory_sp...  16 us

profile of v3, /device:TPU:0, one launch (start us, length us, event | category | flops | bytes accessed | tf_op | source)
XLA Modules:
  0.0 33.6 jit_solution(17080697266909266572)
XLA Ops:
  0.6 16.0 %shard_map.94 = (bf16[2,1,5,2,64,128]{5,4,3,2,1,0:T(8,128)(2,1)}, bf16[2,1,2,128,128]{4,3,2,1,0:T(8,128)(2,1)}, bf16[1,1,2,128,128]{4,3,2,1,0:T(8,128)(2,1)}) custom-call(bf16[2,1,2,128,128]{4,3,2,1,0:T(8,128)(2,1)} %self_hbm.1, bf16[2,1,4,2,128,128]{5,4,3,2,1,0:T(8,128)(2,1)} %coup_hbm.1, s32[2,1,64]{2,1,0:T(1,128)} %skel_hbm.1, s32[2,1,64]{2,1,0:T(1,128)} %red_hbm.1, ...), custom_call_target="tpu_custom_call" | custom-call | tf_op jit(solution)/shard_map/pallas_call | solution.py:292
  16.6 17.0 %shard_map.95 = (bf16[2,1,5,2,64,128]{5,4,3,2,1,0:T(8,128)(2,1)}, bf16[2,1,2,128,128]{4,3,2,1,0:T(8,128)(2,1)}, bf16[1,1,2,128,128]{4,3,2,1,0:T(8,128)(2,1)}) custom-call(bf16[2,1,5,2,64,128]{5,4,3,2,1,0:T(8,128)(2,1)} %get-tuple-element.6.refs_0_, bf16[2,1,2,128,128]{4,3,2,1,0:T(8,128)(2,1)} %get-tuple-element.7.refs_1_, ...), custom_call_target="tpu_custom_call" | custom-call | tf_op jit(solution)/shard_map/pallas_call | solution.py:332

commit v4 on v3

--- a/solution.py
+++ b/solution.py
@@ -291,7 +291,7 @@
     )
     made = pl.pallas_call(
         kernel,
-        out_shape=shapes,
+        out_shape=tuple(pltpu.VMEM(shape.shape, shape.dtype) for shape in shapes),
         in_specs=[pl.BlockSpec(memory_space=pl.ANY)] * 7,
         out_specs=(pl.BlockSpec(memory_space=pl.ANY),) * 3,
         scratch_shapes=[
@@ -335,7 +335,7 @@
         in_specs=[pl.BlockSpec(memory_space=pl.ANY)] * 3,
         out_specs=(pl.BlockSpec(memory_space=pltpu.HBM),) * 3,
         scratch_shapes=[pltpu.SemaphoreType.DMA((3,))],
-        compiler_params=pltpu.CompilerParams(vmem_limit_bytes=62 * 2**20),
+        compiler_params=pltpu.CompilerParams(vmem_limit_bytes=2**20),
     )(*made)
 
 

time: 33.8 us -> 17.5 us (0.52)
  Pallas kernels: 33 us -> 16.7 us
    pallas_call x1, Pallas kernels: 17 us -> 0.81 us  [local(): pl.pallas_call(hand_over, out_shape=shapes, in_specs=[pl.BlockSpec(memory...]
where the time goes in v4:
time: 17.5 us; the launch traced here: 17.3 us
  Pallas kernels  16.7 us (95%)
  between operations  0.64 us (4%)
    pallas_call x1, Pallas kernels, local(): pl.pallas_call(kernel, out_shape=tuple((pltpu.VMEM(shape.shape, shape.dty...  15.9 us
    pallas_call x1, Pallas kernels, local(): pl.pallas_call(hand_over, out_shape=shapes, in_specs=[pl.BlockSpec(memory...  0.81 us

profile of v4, /device:TPU:0, one launch (start us, length us, event | category | flops | bytes accessed | tf_op | source)
XLA Modules:
  0.0 17.3 jit_solution(5341035969940923238)
XLA Ops:
  0.6 15.9 %shard_map.94 = (bf16[2,1,5,2,64,128]{5,4,3,2,1,0:T(8,128)(2,1)S(1)}, bf16[2,1,2,128,128]{4,3,2,1,0:T(8,128)(2,1)S(1)}, bf16[1,1,2,128,128]{4,3,2,1,0:T(8,128)(2,1)S(1)}) custom-call(bf16[2,1,2,128,128]{4,3,2,1,0:T(8,128)(2,1)} %self_hbm.1, bf16[2,1,4,2,128,128]{5,4,3,2,1,0:T(8,128)(2,1)} %coup_hbm.1, s32[2,1,64]{2,1,0:T(1,128)} %skel_hbm.1, ...), custom_call_target="tpu_custom_call" | custom-call | tf_op jit(solution)/shard_map/pallas_call | solution.py:292
  16.5 0.8 %shard_map.95 = (bf16[2,1,5,2,64,128]{5,4,3,2,1,0:T(8,128)(2,1)}, bf16[2,1,2,128,128]{4,3,2,1,0:T(8,128)(2,1)}, bf16[1,1,2,128,128]{4,3,2,1,0:T(8,128)(2,1)}) custom-call(bf16[2,1,5,2,64,128]{5,4,3,2,1,0:T(8,128)(2,1)S(1)} %get-tuple-element.6.refs_0_, bf16[2,1,2,128,128]{4,3,2,1,0:T(8,128)(2,1)S(1)} %get-tuple-element.7.refs_1_, ...), custom_call_target="tpu_custom_call" | custom-call | tf_op jit(solution)/shard_map/pallas_call | solution.py:332

commit v5 on v4

--- a/solution.py
+++ b/solution.py
@@ -147,58 +147,71 @@
     send_par_y.start()
     send_par_x.start()
 
-    for j in range(n):
-        for copy in large[j]:
+    for pair in large:
+        for copy in pair:
             copy.wait()
     params = [read_params(par[j]) for j in range(n)]
-    w_right = []
-    for j in range(n):
-        right_ops = cat(1, above(coup, j, 2), above(coup, j, 0), above(own, j))
-        made = factors(params[j], right_ops)
-        f_up, f_right, f_own = (made[:, k * points : (k + 1) * points] for k in range(3))
-        put_factor(j, 4, f_up)
-        put_factor(j, 2, f_right)
-        put_factor(j, 0, f_own)
-        own_rows = dot(pick[j], beside(own, j)).astype(BF16)
-        left_ops = cat(0, beside(coup, j, 3), beside(coup, j, 1), own_rows)
-        ends = dot_nt(left_ops, params[j][1]).astype(BF16)
-        w_send_y[j] = dot(folded(ends[:points]), f_up).astype(BF16)
-        send_w_y[j].start()
-        w_right.append(dot(folded(ends[points : 2 * points]), f_right))
-        if j == n - 1:
-            w_send_x[...] = w_right[j].astype(BF16)
-            send_w_x.start()
-        e_mix = folded(ends[2 * points :])
-        self_term[j] = dot(e_mix, cat(1, f_own, f_up))
-        extra[j, :size, :] = cat(1, e_mix[:size, :size], e_mix[size:, :size])
-        extra[j, size:, :] = pick[j]
-        acc[j] = above(own, j).astype(F32)
-        if j > 0:
-            acc[j] = acc[j] - w_right[j - 1]
-
-    @pl.when(odd == 1)
-    def _():
-        send_extra.start()
-
-    for j in range(n):
-        for k in (0, 2, 4):
-            store(fac.at[j, k], factor_out.at[j, 0, k])
+    made = [
+        factors(params[j], cat(1, above(coup, j, 2), above(coup, j, 0), above(own, j)))
+        for j in range(n)
+    ]
+    ends = [
+        dot_nt(cat(0, beside(coup, j, 3), beside(coup, j, 1)), params[j][1]).astype(BF16)
+        for j in range(n)
+    ]
+    f_up, f_right, f_own = (
+        [made[j][:, k * points : (k + 1) * points] for j in range(n)] for k in range(3)
+    )
+    w_up = [dot(folded(ends[j][:points]), f_up[j]) for j in range(n)]
+    w_right = [dot(folded(ends[j][points:]), f_right[j]) for j in range(n)]
+    for j in range(n):
+        w_send_y[j] = w_up[j].astype(BF16)
+    w_send_x[...] = w_right[n - 1].astype(BF16)
+    for copy in send_w_y:
+        copy.start()
+    send_w_x.start()
 
     def from_next(next_params, j, k):
         made = factors(next_params, above(coup, j, k))
         put_factor(j, k, made)
         ends = dot_nt(beside(coup, j, k - 1), next_params[1]).astype(BF16)
-        return made, dot(folded(ends), made)
-
+        return dot(folded(ends), made)
+
+    for j in range(n):
+        put_factor(j, 4, f_up[j])
+        put_factor(j, 2, f_right[j])
+        put_factor(j, 0, f_own[j])
+        own_rows = dot(pick[j], beside(own, j)).astype(BF16)
+        e_mix = folded(dot_nt(own_rows, params[j][1]).astype(BF16))
+        self_term[j] = dot(e_mix, cat(1, f_own[j], f_up[j]))
+        extra[j, :size, :] = cat(1, e_mix[:size, :size], e_mix[size:, :size])
+        extra[j, size:, :] = pick[j]
+        block = above(own, j).astype(F32)
+        if j > 0:
+            block = block - w_right[j - 1]
+        if j < n - 1:
+            block = block - from_next(params[j + 1], j, 1)
+        acc[j] = block
+
+    @pl.when(odd == 1)
+    def _():
+        send_extra.start()
+
+    for j in range(n):
+        for k in (0, 2, 4):
+            store(fac.at[j, k], factor_out.at[j, 0, k])
     for j in range(n - 1):
-        acc[j] = acc[j] - from_next(params[j + 1], j, 1)[1]
         store(fac.at[j, 1], factor_out.at[j + 1, 0, 1])
+
     send_par_y.wait_recv()
-    for j in range(n):
-        acc[j] = acc[j] - from_next(read_params(par_y[j]), j, 3)[1]
-        send_fac_y[j].start()
     send_par_x.wait_recv()
-    acc[n - 1] = acc[n - 1] - from_next(read_params(par_x[...]), n - 1, 1)[1]
+    y_params = [read_params(par_y[j]) for j in range(n)]
+    gained = [from_next(y_params[j], j, 3) for j in range(n)]
+    gained[n - 1] = gained[n - 1] + from_next(read_params(par_x[...]), n - 1, 1)
+    for j in range(n):
+        acc[j] = acc[j] - gained[j]
+    for copy in send_fac_y:
+        copy.start()
     send_fac_x.start()
 
     @pl.when(odd == 0)

time: 17.5 us -> 17.7 us (1.011)
  Pallas kernels: 16.7 us -> 16.9 us
    pallas_call x1, Pallas kernels: 15.9 us -> 16.1 us  [local(): pl.pallas_call(kernel, out_shape=tuple((pltpu.VMEM(shape.shape, shape.dty...]
where the time goes in v5:
time: 17.7 us; the launch traced here: 17.5 us
  Pallas kernels  16.9 us (95%)
  between operations  0.64 us (4%)
    pallas_call x1, Pallas kernels, local(): pl.pallas_call(kernel, out_shape=tuple((pltpu.VMEM(shape.shape, shape.dty...  16.1 us
    pallas_call x1, Pallas kernels, local(): pl.pallas_call(hand_over, out_shape=shapes, in_specs=[pl.BlockSpec(memory...  0.81 us

profile of v5, /device:TPU:0, one launch (start us, length us, event | category | flops | bytes accessed | tf_op | source)
XLA Modules:
  0.0 17.5 jit_solution(15600989858163583180)
XLA Ops:
  0.6 16.1 %shard_map.94 = (bf16[2,1,5,2,64,128]{5,4,3,2,1,0:T(8,128)(2,1)S(1)}, bf16[2,1,2,128,128]{4,3,2,1,0:T(8,128)(2,1)S(1)}, bf16[1,1,2,128,128]{4,3,2,1,0:T(8,128)(2,1)S(1)}) custom-call(bf16[2,1,2,128,128]{4,3,2,1,0:T(8,128)(2,1)} %self_hbm.1, bf16[2,1,4,2,128,128]{5,4,3,2,1,0:T(8,128)(2,1)} %coup_hbm.1, s32[2,1,64]{2,1,0:T(1,128)} %skel_hbm.1, ...), custom_call_target="tpu_custom_call" | custom-call | tf_op jit(solution)/shard_map/pallas_call | solution.py:305
  16.7 0.8 %shard_map.95 = (bf16[2,1,5,2,64,128]{5,4,3,2,1,0:T(8,128)(2,1)}, bf16[2,1,2,128,128]{4,3,2,1,0:T(8,128)(2,1)}, bf16[1,1,2,128,128]{4,3,2,1,0:T(8,128)(2,1)}) custom-call(bf16[2,1,5,2,64,128]{5,4,3,2,1,0:T(8,128)(2,1)S(1)} %get-tuple-element.6.refs_0_, bf16[2,1,2,128,128]{4,3,2,1,0:T(8,128)(2,1)S(1)} %get-tuple-element.7.refs_1_, ...), custom_call_target="tpu_custom_call" | custom-call | tf_op jit(solution)/shard_map/pallas_call | solution.py:345

commit v6 on v5

--- a/solution.py
+++ b/solution.py
@@ -74,7 +74,7 @@
     factor_out, updated_out, coarse_out,
     own, coup, skel, red, interp, pivot, inverse,
     pick, par, par_x, par_y, extra, extra_y, fac, acc, w_send_x, w_send_y, w_x, w_y,
-    self_term, keep_k, g_own, g_other, updated, coarse,
+    self_term, k_own, keep_k, g_own, g_other, updated, coarse,
     in_sem, send_sem, recv_sem, out_sem,
 ):
     n, points = own.shape[0], own.shape[2]
@@ -128,7 +128,7 @@
     send_par_y = remote(par, par_y, 1, y_back)
     send_extra = remote(extra, extra_y, 2, y_back)
     send_w_x = remote(w_send_x, w_x, 3, x_next)
-    send_k = remote(keep_k.at[pl.ds(half, half)], keep_k.at[pl.ds(0, half)], 4, partner)
+    send_k = remote(k_own.at[pl.ds((1 - odd) * half, half)], keep_k, 4, partner)
     send_g = remote(g_own.at[pl.ds((1 - odd) * half, half)], g_other, 5, partner)
     send_fac_x = remote(fac.at[n - 1, 1], factor_out.at[0, 0, 1], 6, x_next)
     send_w_y = [remote(w_send_y.at[j], w_y.at[j], 7 + 2 * j, y_next) for j in range(n)]
@@ -193,9 +193,7 @@
             block = block - from_next(params[j + 1], j, 1)
         acc[j] = block
 
-    @pl.when(odd == 1)
-    def _():
-        send_extra.start()
+    send_extra.start()
 
     for j in range(n):
         for k in (0, 2, 4):
@@ -214,24 +212,21 @@
         copy.start()
     send_fac_x.start()
 
-    @pl.when(odd == 0)
-    def _():
-        send_extra.wait_recv()
-        for j in reversed(range(n)):
-            lower_pick, upper_pick = pick[j], extra_y[j, size:, :]
-            rows = folded(dot(lower_pick, beside(coup, j, 2))) - self_term[j, :, points:]
-            keep_k[j, 0] = paired(dot_nt(rows.astype(BF16), upper_pick).astype(BF16))
-            end = extra_y[j, :size, :]
-            e_re, e_im = end[:, :size], end[:, size:]
-            e_mix = cat(0, cat(1, e_re, -e_im), cat(1, e_im, e_re))
-            upper_factor = above(fac, j, 3)
-            rows = folded(dot(upper_pick, beside(coup, j, 3))) - dot(e_mix, upper_factor)
-            keep_k[j, 1] = paired(dot_nt(rows.astype(BF16), lower_pick).astype(BF16))
-        send_k.start()
-
+    send_extra.wait_recv()
     send_w_x.wait_recv()
-    for j in range(n):
-        send_w_y[j].wait_recv()
+    for copy in send_w_y:
+        copy.wait_recv()
+
+    for j in range(n):
+        lower_pick, upper_pick = pick[j], extra_y[j, size:, :]
+        rows = folded(dot(lower_pick, beside(coup, j, 2))) - self_term[j, :, points:]
+        k_own[j, 0] = paired(dot_nt(rows.astype(BF16), upper_pick).astype(BF16))
+        end = extra_y[j, :size, :]
+        e_re, e_im = end[:, :size], end[:, size:]
+        e_mix = cat(0, cat(1, e_re, -e_im), cat(1, e_im, e_re))
+        rows = folded(dot(upper_pick, beside(coup, j, 3))) - dot(e_mix, above(fac, j, 3))
+        k_own[j, 1] = paired(dot_nt(rows.astype(BF16), lower_pick).astype(BF16))
+
     for j in range(n):
         total = acc[j] - w_y[j].astype(F32)
         if j == 0:
@@ -244,19 +239,17 @@
         rows = (folded(rows) - self_term[j, :, :points]).astype(BF16)
         g_own[j] = paired(dot_nt(rows, pick[j]).astype(BF16))
     send_g.start()
+    send_k.start()
     for j in range(n):
         store(updated.at[j], updated_out.at[j, 0])
 
-    @pl.when(odd == 1)
-    def _():
-        send_k.wait_recv()
-
+    send_k.wait_recv()
     send_g.wait_recv()
     for t in range(half):
         mine, other = g_own[odd * half + t], g_other[t]
         lower = jnp.where(odd == 0, mine, other)
         upper = jnp.where(odd == 0, other, mine)
-        k_lower, k_upper = keep_k[t, 0], keep_k[t, 1]
+        k_lower, k_upper = (jnp.where(odd == 0, k_own[t, k], keep_k[t, k]) for k in range(2))
         for c in range(2):
             part = slice(c * size, (c + 1) * size)
             coarse[t, c, :size, :] = cat(1, lower[:, part], k_lower[:, part])
@@ -266,16 +259,8 @@
     send_fac_x.wait_recv()
     for copy in send_fac_y:
         copy.wait_recv()
-    for copy in [send_par_x, send_par_y, send_w_x, send_g, send_fac_x, *send_w_y, *send_fac_y]:
+    for copy in [send_par_x, send_par_y, send_w_x, send_extra, send_k, send_g, send_fac_x, *send_w_y, *send_fac_y]:
         copy.wait_send()
-
-    @pl.when(odd == 1)
-    def _():
-        send_extra.wait_send()
-
-    @pl.when(odd == 0)
-    def _():
-        send_k.wait_send()
 
     for copy in outs:
         copy.wait()
@@ -329,6 +314,7 @@
             vmem((n, 2 * points, points), BF16),
             vmem((n, 2 * size, 2 * points), F32),
             vmem((n, 2, size, 2 * size), BF16),
+            vmem((half, 2, size, 2 * size), BF16),
             vmem((n, size, 2 * size), BF16),
             vmem((half, size, 2 * size), BF16),
             vmem((n, 2, points, points), BF16),

time: 17.7 us -> 17.7 us (level)
  no operation moved by 1% of the time
where the time goes in v6:
time: 17.7 us; the launch traced here: 17.5 us
  Pallas kernels  16.9 us (95%)
  between operations  0.64 us (4%)
    pallas_call x1, Pallas kernels, local(): pl.pallas_call(kernel, out_shape=tuple((pltpu.VMEM(shape.shape, shape.dty...  16.1 us
    pallas_call x1, Pallas kernels, local(): pl.pallas_call(hand_over, out_shape=shapes, in_specs=[pl.BlockSpec(memory...  0.81 us

profile of v6, /device:TPU:0, one launch (start us, length us, event | category | flops | bytes accessed | tf_op | source)
XLA Modules:
  0.0 17.5 jit_solution(6656055990669598745)
XLA Ops:
  0.6 16.1 %shard_map.94 = (bf16[2,1,5,2,64,128]{5,4,3,2,1,0:T(8,128)(2,1)S(1)}, bf16[2,1,2,128,128]{4,3,2,1,0:T(8,128)(2,1)S(1)}, bf16[1,1,2,128,128]{4,3,2,1,0:T(8,128)(2,1)S(1)}) custom-call(bf16[2,1,2,128,128]{4,3,2,1,0:T(8,128)(2,1)} %self_hbm.1, bf16[2,1,4,2,128,128]{5,4,3,2,1,0:T(8,128)(2,1)} %coup_hbm.1, s32[2,1,64]{2,1,0:T(1,128)} %skel_hbm.1, ...), custom_call_target="tpu_custom_call" | custom-call | tf_op jit(solution)/shard_map/pallas_call | solution.py:290
  16.7 0.8 %shard_map.95 = (bf16[2,1,5,2,64,128]{5,4,3,2,1,0:T(8,128)(2,1)}, bf16[2,1,2,128,128]{4,3,2,1,0:T(8,128)(2,1)}, bf16[1,1,2,128,128]{4,3,2,1,0:T(8,128)(2,1)}) custom-call(bf16[2,1,5,2,64,128]{5,4,3,2,1,0:T(8,128)(2,1)S(1)} %get-tuple-element.6.refs_0_, bf16[2,1,2,128,128]{4,3,2,1,0:T(8,128)(2,1)S(1)} %get-tuple-element.7.refs_1_, ...), custom_call_target="tpu_custom_call" | custom-call | tf_op jit(solution)/shard_map/pallas_call | solution.py:331
